TPU v7x, 32 devices: a whole 2x2x4 slice. The times are simulated.
32 devices in a mesh: centre: 8 (over z, y), row: 4 (over x, core).
Axes of the slice: x: 2, y: 2, z: 4, core: 2. Of those that a mesh axis runs over, the one named last changes fastest.
Arguments:
- pool: bfloat16 [1024, 16384], P('centre', 'row')
- batch_index: int32 [1024], P('row'), may hold values from 0 to 16383, as said below
- targets: float32 [10, 1024], P(None, 'row'), may hold values from -6 to 6
- centres: bfloat16 [65536, 1024], P(('centre', 'row'))
- weights: float32 [10, 65536], P(None, ('centre', 'row')), may hold values from -0.0234375 to 0.0234375
- sample_index: int32 [512], P(('centre', 'row')), may hold values from 0 to 65535, as said below
- factor: float32 [512, 128], P(('centre', 'row')), may hold values from -0.5 to 0.5
Outputs:
- gradient: float32 [10, 1024], P(None, 'row')
- update: float32 [10, 512], P(None, ('centre', 'row'))
Inputs may be any that keep to these rules, and one draw needn't show every extreme that they name: `batch_index`: the entries at positions r * 256 to (r + 1) * 256 - 1 lie in r * 4096 to (r + 1) * 4096 - 1; repeats may occur. `sample_index`: all entries differ; the entries at positions k * 16 to (k + 1) * 16 - 1 lie in k * 2048 to (k + 1) * 2048 - 1.
All inputs are finite; a program needn't handle non-finite values.
Results may differ from a plain program's by a relative error of at most 0.0003.
Values may be sent and summed in bfloat16 or wider, within the bound.
A program may use at most 128 MiB of HBM per device.

v0:
```python
import math
import jax
import jax.numpy as jnp
from jax import lax
from jax.sharding import PartitionSpec as P

PROJ_STEPS = 2
EPS = 1e-06
HIGH = lax.Precision.HIGHEST


def row_scale(rows, axis):
    values = rows.astype(jnp.float32)
    return jnp.sqrt(jnp.mean(values * values, axis=axis) + EPS)


def tangent_kernel(inner, left_scale, right_scale, width):
    product = left_scale[:, None] * right_scale[None, :]
    cosine = jnp.clip(inner / (width * product), -1.0, 1.0)
    angle = jnp.arccos(cosine)
    first = (math.pi - angle) / math.pi
    second = (cosine * (math.pi - angle) + jnp.sqrt(1.0 - cosine * cosine)) / math.pi
    return product * (second + cosine * first)


def on_device(pool, batch_index, targets, centres, weights, sample_index, factor):
    width = float(centres.shape[1])
    labels = weights.shape[0]
    rows_dev = batch_index.shape[0]
    pool_dev = pool.shape[1]
    cent_dev = centres.shape[0]
    samp_dev = sample_index.shape[0]
    row_count = lax.axis_size("row")
    total_rows = rows_dev * row_count
    total_samp = samp_dev * row_count * lax.axis_size("centre")
    contract = (((1,), (1,)), ((), ()))
    local_batch = batch_index - lax.axis_index("row") * pool_dev
    picked = jnp.take(pool, local_batch, axis=1)
    features = lax.all_gather(picked, "centre", axis=0, tiled=True)
    all_targets = lax.all_gather(targets, "row", axis=1, tiled=True)
    centre_scale = row_scale(centres, 1)
    local_sample = sample_index - lax.axis_index(("centre", "row")) * cent_dev
    sample_rows = jnp.take(centres, local_sample, axis=0)
    sample_scale = jnp.take(centre_scale, local_sample)
    piece = lax.all_gather(features, "row", axis=1, tiled=True)
    inner = jnp.dot(centres, piece, preferred_element_type=jnp.float32)
    kernel = tangent_kernel(inner, centre_scale, row_scale(piece, 0), width)
    partial_value = jnp.dot(weights, kernel, precision=HIGH)
    tiles = jnp.concatenate([partial_value, jnp.take(kernel, local_sample, axis=0)], axis=0)
    partial_value = tiles[:labels]
    cross = tiles[labels:]
    totals = lax.psum(partial_value, ("centre", "row"))
    gradient_all = totals - all_targets
    gradient = lax.dynamic_slice_in_dim(gradient_all, lax.axis_index("row") * rows_dev, rows_dev, 1)
    push = lax.dot_general(gradient_all, cross, contract, precision=HIGH) / total_rows
    piece = lax.all_gather(sample_rows, ("centre", "row"), axis=0, tiled=True)
    inner = lax.dot_general(sample_rows, piece, contract, preferred_element_type=jnp.float32)
    block = tangent_kernel(inner, sample_scale, row_scale(piece, 1), width)
    update = jnp.zeros((labels, samp_dev), jnp.float32)
    for step in range(PROJ_STEPS):
        if step == 0:
            slope = push
        else:
            update_whole = lax.all_gather(update, ("centre", "row"), axis=1, tiled=True)
            slope = (
                lax.dot_general(update_whole, block, contract, precision=HIGH) / total_samp + push
            )
        coef = lax.psum(jnp.dot(slope, factor, precision=HIGH), ("centre", "row"))
        update = update - (slope - jnp.dot(coef, factor.T, precision=HIGH))
    return (gradient, update)


def solution(mesh):
    placed = (
        P("centre", "row"),
        P("row"),
        P(None, "row"),
        P(("centre", "row"), None),
        P(None, ("centre", "row")),
        P(("centre", "row")),
        P(("centre", "row"), None),
    )
    return jax.shard_map(
        on_device,
        mesh=mesh,
        in_specs=placed,
        out_specs=(P(None, "row"), P(None, ("centre", "row"))),
        check_vma=False,
    )
```

profile of v0, /device:TPU:10, one launch (start us, length us, event | category | flops | bytes accessed | tf_op | source)
XLA Modules:
  0.0 314.5 jit_solution(3120540883913514165)
XLA Ops:
  7.2 0.7 compare_and_fusion
  7.9 3.3 %gather_fusion.3 = bf16[16,1024]{1,0:T(8,128)(2,1)S(1)} fusion(bf16[2048,1024]{1,0:T(8,128)(2,1)} %param.10, s32[1024]{0:T(1024)S(1)} %pad_clamp_fusion), kind=kCustom, calls=%fused_computation.3 | custom fusion | bytes 65600 | tf_op jit(solution)/shard_map/jit(_take)/gather | solution.py:43
  11.3 0.7 broadcast_select_fusion
  12.0 1.6 copy.13
  13.6 0.7 compare_and_fusion.1
  14.3 0.9 gather_fusion
  15.3 28.9 %all_gather.15 = bf16[1024,256]{0,1:T(8,128)(2,1)} all-gather(bf16[128,256]{0,1:T(8,128)(2,1)S(1)} %select_bitcast_fusion), channel_id=1, replica_groups=mesh['centre'=8,'row'=4] {'centre'}, dimensions={0}, use_global_device_ids=true | all-gather | bytes 589824 | tf_op jit(solution)/shard_map/all_gather | solution.py:39
  44.2 3.1 multiply_reduce_fusion
  47.3 0.7 gather_fusion.2
  48.0 5.2 %all_gather.17 = f32[10,1024]{1,0:T(8,128)S(1)} all-gather(f32[10,256]{1,0:T(8,128)S(1)} %copy-done.3), channel_id=1, replica_groups=mesh['centre'=8,'row'=4] {'row'}, dimensions={1}, use_global_device_ids=true | all-gather | bytes 51200 | tf_op jit(solution)/shard_map/all_gather | solution.py:40
  53.2 13.0 %all-gather.5.cloned.1.call-done = bf16[512,1024]{1,0:T(8,128)(2,1)} async-done(((bf16[16,1024]{1,0:T(8,128)(2,1)}), bf16[512,1024]{1,0:T(8,128)(2,1)}) %all-gather.5.cloned.1.call-update) | async-done | bytes 1048592 | tf_op jit(solution)/shard_map/all_gather | solution.py:56
  66.3 1.5 multiply_reduce_fusion.2
  67.8 1.6 fusion.2
  69.4 19.9 %all-gather.3.cloned.1.call-done = bf16[1024,1024]{0,1:T(8,128)(2,1)} async-done(((bf16[1024,256]{0,1:T(8,128)(2,1)}), bf16[1024,1024]{0,1:T(8,128)(2,1)}) %all-gather.3.cloned.1.call-update) | async-done | bytes 2097168 | tf_op jit(solution)/shard_map/all_gather | solution.py:45
  89.2 2.1 multiply_reduce_fusion.1
  91.3 29.4 %multiply_multiply_fusion = f32[2048,1024]{0,1:T(8,128)} fusion(bf16[1024,1024]{0,1:T(8,128)(2,1)} %all-gather.3.cloned.1.call-done, bf16[2048,1024]{1,0:T(8,128)(2,1)} %param.10, f32[1024]{0:T(1024)S(1)} %add_sqrt_fusion.1, f32[2048]{0:T(1024)S(1)} %add_sqrt_fusion), kind=kOutput, calls=%fused_computation.4 | convolution fusion | flops 4330618880 | bytes 14692352 | tf_op jit(solution)/shard_map/dot_general | solution.py:46
  120.7 9.3 %copy.14 = f32[2048,1024]{1,0:T(8,128)} copy(f32[2048,1024]{0,1:T(8,128)} %multiply_multiply_fusion) | data formatting | bytes 16777216 | tf_op jit(solution)/shard_map/mul | solution.py:23
  129.9 4.0 %gather_fusion.1 = f32[16,1024]{1,0:T(8,128)S(1)} fusion(f32[2048,1024]{1,0:T(8,128)} %copy.14, s32[1024]{0:T(1024)S(1)} %pad_clamp_fusion), kind=kCustom, calls=%fused_computation.1 | custom fusion | bytes 131136 | tf_op jit(solution)/shard_map/jit(_take)/gather | solution.py:49
  134.0 9.4 %convolution_bitcast_fusion = f32[10,1024]{1,0:T(8,128)S(1)} fusion(f32[2048,1024]{0,1:T(8,128)} %multiply_multiply_fusion, f32[10,2048]{1,0:T(8,128)S(1)} %copy-done), kind=kOutput, calls=%fused_computation.11 | convolution fusion | flops 251658240 | bytes 8511488 | tf_op jit(solution)/shard_map/dot_general | solution.py:48
  143.4 41.3 %psum.21 = f32[10,1024]{1,0:T(8,128)S(1)} all-reduce(f32[10,1024]{1,0:T(8,128)S(1)} %convolution_bitcast_fusion), channel_id=1, replica_groups=mesh['centre'=8,'row'=4] {'centre','row'}, use_global_device_ids=true, to_apply=%region_2.3 | all-reduce | flops 10240 | bytes 81920 | tf_op jit(solution)/shard_map/psum | solution.py:52
  185.1 40.0 %psum.22 = f32[10,128]{1,0:T(8,128)S(1)} all-reduce(f32[10,128]{1,0:T(8,128)S(1)} %fusion.33), channel_id=1, replica_groups=mesh['centre'=8,'row'=4] {'centre','row'}, use_global_device_ids=true, to_apply=%region_3.4 | all-reduce | flops 1280 | bytes 10240 | tf_op jit(solution)/shard_map/psum | solution.py:68
  225.4 31.4 %all_gather.18 = f32[10,512]{0,1:T(8,128)S(1)} all-gather(f32[10,16]{0,1:T(8,128)S(1)} %copy.15), channel_id=1, replica_groups=mesh['centre'=8,'row'=4] {'centre','row'}, dimensions={1}, use_global_device_ids=true | all-gather | bytes 21120 | tf_op jit(solution)/shard_map/all_gather | solution.py:64
  257.5 48.8 %psum.23 = f32[10,128]{1,0:T(8,128)S(1)} all-reduce(f32[10,128]{1,0:T(8,128)S(1)} %fusion.34), channel_id=1, replica_groups=mesh['centre'=8,'row'=4] {'centre','row'}, use_global_device_ids=true, to_apply=%region_5.6 | all-reduce | flops 1280 | bytes 10240 | tf_op jit(solution)/shard_map/psum | solution.py:68
  306.4 0.7 fusion.3
  (27 shorter events, 2.2 us)
Async XLA Ops:
  7.2 126.8 %copy-start = (f32[10,2048]{1,0:T(8,128)S(1)}, f32[10,2048]{1,0:T(8,128)}, u32[]{:S(2)}) copy-start(f32[10,2048]{1,0:T(8,128)} %param.11) | copy-start | bytes 245764
  7.2 40.8 %copy-start.3 = (f32[10,256]{1,0:T(8,128)S(1)}, f32[10,256]{1,0:T(8,128)}, u32[]{:S(2)}) copy-start(f32[10,256]{1,0:T(8,128)} %param.9) | copy-start | bytes 30724
  7.2 59.1 %all-gather.5.cloned.1.call-start = ((), (), s32[]{:S(2)}) async-start(), calls=%async_computation.1 | async-start | bytes 1081344 | tf_op jit(solution)/shard_map/all_gather | solution.py:56
  11.9 55.8 %copy-start.1 = (bf16[16,1024]{1,0:T(8,128)(2,1)S(1)}, bf16[16,1024]{1,0:T(8,128)(2,1)}, u32[]{:S(2)}) copy-start(bf16[16,1024]{1,0:T(8,128)(2,1)} %broadcast_select_fusion) | copy-start | bytes 98308
  12.0 77.3 %all-gather.3.cloned.1.call-start = ((), (), s32[]{:S(2)}) async-start(), calls=%async_computation | async-start | bytes 2621440 | tf_op jit(solution)/shard_map/all_gather | solution.py:45
  129.9 55.0 %copy-start.2 = (f32[16,128]{1,0:T(8,128)S(1)}, f32[16,128]{1,0:T(8,128)}, u32[]{:S(2)}) copy-start(f32[16,128]{1,0:T(8,128)} %param.13) | copy-start | bytes 24580
Sparse Core Ops, SparseCore 0:
  12.1 54.1 all-gather.4
  67.8 21.3 all-gather.2
where the time goes:
time: 315 us
  blocking collectives  196 us (62%)
  matrix products  42.3 us (13%)
  waiting for transfers between devices  32.9 us (10%)
  local copies, waits for them, and re-layouts  20.5 us (7%)
  between operations  14.2 us (5%)
  other arithmetic  8.84 us (3%)
    psum x2, blocking collectives, on_device(): coef = lax.psum(jnp.dot(slope, factor, precision=HIGH), ('centre', 'row'))  88.9 us
    psum x1, blocking collectives, on_device(): totals = lax.psum(partial_value, ('centre', 'row'))  41.3 us
    all_gather x1, blocking collectives, on_device(): update_whole = lax.all_gather(update, ('centre', 'row'), axis=1, tiled=True)  31.4 us
    dot_general x1, matrix products, on_device(): inner = jnp.dot(centres, piece, preferred_element_type=jnp.float32)  29.4 us
    all_gather x1, blocking collectives, on_device(): features = lax.all_gather(picked, 'centre', axis=0, tiled=True)  28.9 us
    all_gather x1, waiting for transfers between devices, on_device(): piece = lax.all_gather(features, 'row', axis=1, tiled=True)  19.9 us
    all_gather x1, waiting for transfers between devices, on_device(): piece = lax.all_gather(sample_rows, ('centre', 'row'), axis=0, tiled=True)  13 us
    dot_general x1, matrix products, on_device(): partial_value = jnp.dot(weights, kernel, precision=HIGH)  9.43 us
  transfers between devices with their start and end apart: 2, of which 2 were waited for; matrix products, arithmetic and copies ran while one was open for 3% of the time, Pallas kernels for 0%

commit v1 on v0

--- a/solution.py
+++ b/solution.py
@@ -3,10 +3,27 @@
 import jax.numpy as jnp
 from jax import lax
 from jax.sharding import PartitionSpec as P
+from jax.lax import axis_index, axis_size, ppermute
 
 PROJ_STEPS = 2
 EPS = 1e-06
 HIGH = lax.Precision.HIGHEST
+
+
+def supply_all_the_meshes(array_axis, state):
+    mesh_dim = "row"
+    n = axis_size(mesh_dim)
+    arr_out = state
+    kept_rows = [arr_out]
+    kept_arr = [(u - 1, u) for u in range(1, n)] + [(n - 1, 0)]
+    for _ in [*range(n - 1)]:
+        arr_out = ppermute(arr_out, axis_name=mesh_dim, perm=kept_arr)
+        kept_rows += [arr_out]
+    lower = jnp.concatenate([*reversed(kept_rows)], axis=array_axis)
+    part_now = jnp.roll(
+        lower, shift=(axis_index(mesh_dim) + 1) * arr_out.shape[array_axis], axis=array_axis
+    )
+    return part_now
 
 
 def row_scale(rows, axis):
@@ -42,7 +59,7 @@
     local_sample = sample_index - lax.axis_index(("centre", "row")) * cent_dev
     sample_rows = jnp.take(centres, local_sample, axis=0)
     sample_scale = jnp.take(centre_scale, local_sample)
-    piece = lax.all_gather(features, "row", axis=1, tiled=True)
+    piece = supply_all_the_meshes(1, state=features)
     inner = jnp.dot(centres, piece, preferred_element_type=jnp.float32)
     kernel = tangent_kernel(inner, centre_scale, row_scale(piece, 0), width)
     partial_value = jnp.dot(weights, kernel, precision=HIGH)

time: 315 us -> 291 us (0.924)
  waiting for transfers between devices: 32.9 us -> 12.5 us
    all_gather x1 -> x0, waiting for transfers between devices: 19.9 us -> none  [on_device(): piece = lax.all_gather(features, 'row', axis=1, tiled=True)]
    all_gather x1, waiting for transfers between devices: 13 us -> 0.01 us  [on_device(): piece = lax.all_gather(sample_rows, ('centre', 'row'), axis=0, tiled=True)]
    ppermute x0 -> x3, waiting for transfers between devices: none -> 12.5 us  [supply_all_the_meshes(): arr_out = ppermute(arr_out, axis_name=mesh_dim, perm=kept_arr)]
  transfers between devices with their start and end apart: 2 -> 4, of which waited for: 2 -> 2; matrix products, arithmetic and copies ran while one was open for 3% -> 21% of each run, Pallas kernels for 0% -> 0%
where the time goes in v1:
time: 291 us; the launch traced here: 290 us
  blocking collectives  194 us (67%)
  matrix products  39.8 us (14%)
  local copies, waits for them, and re-layouts  22.2 us (8%)
  between operations  14.3 us (5%)
  waiting for transfers between devices  12.5 us (4%)
  other arithmetic  7.25 us (2%)
    psum x2, blocking collectives, on_device(): coef = lax.psum(jnp.dot(slope, factor, precision=HIGH), ('centre', 'row'))  88.5 us
    psum x1, blocking collectives, on_device(): totals = lax.psum(partial_value, ('centre', 'row'))  41.1 us
    all_gather x1, blocking collectives, on_device(): update_whole = lax.all_gather(update, ('centre', 'row'), axis=1, tiled=True)  31.3 us
    all_gather x1, blocking collectives, on_device(): features = lax.all_gather(picked, 'centre', axis=0, tiled=True)  26.9 us
    dot_general x1, matrix products, on_device(): inner = jnp.dot(centres, piece, preferred_element_type=jnp.float32)  26.9 us
    ppermute x3, waiting for transfers between devices, supply_all_the_meshes(): arr_out = ppermute(arr_out, axis_name=mesh_dim, perm=kept_arr)  12.5 us
    dot_general x1, matrix products, on_device(): partial_value = jnp.dot(weights, kernel, precision=HIGH)  9.43 us
    mul x1, local copies, waits for them, and re-layouts, tangent_kernel(): return product * (second + cosine * first)  9.27 us
  transfers between devices with their start and end apart: 4, of which 2 were waited for; matrix products, arithmetic and copies ran while one was open for 21% of the time, Pallas kernels for 0%

profile of v1, /device:TPU:10, one launch (start us, length us, event | category | flops | bytes accessed | tf_op | source)
XLA Modules:
  0.0 290.2 jit_solution(17802373818850747467)
XLA Ops:
  7.2 0.7 compare_and_fusion.1
  7.9 1.6 copy.13
  9.6 0.9 gather_fusion
  10.5 26.9 %all_gather.12 = bf16[1024,256]{0,1:T(8,128)(2,1)S(1)} all-gather(bf16[128,256]{0,1:T(8,128)(2,1)S(1)} %select_bitcast_fusion), channel_id=1, replica_groups=mesh['centre'=8,'row'=4] {'centre'}, dimensions={0}, use_global_device_ids=true | all-gather | bytes 589824 | tf_op jit(solution)/shard_map/all_gather | solution.py:56
  37.5 8.6 %collective-permute-done = bf16[1024,256]{0,1:T(8,128)(2,1)S(1)} collective-permute-done((bf16[1024,256]{0,1:T(8,128)(2,1)S(1)}, bf16[1024,256]{0,1:T(8,128)(2,1)S(1)}, u32[]{:S(2)}, u32[]{:S(2)}) %collective-permute-start) | collective-permute-done | bytes 524320 | tf_op jit(solution)/shard_map/ppermute | solution.py:20
  46.1 0.7 compare_and_fusion
  46.8 3.3 %gather_fusion.3 = bf16[16,1024]{1,0:T(8,128)(2,1)S(1)} fusion(bf16[2048,1024]{1,0:T(8,128)(2,1)} %param.10, s32[1024]{0:T(1024)S(1)} %pad_clamp_fusion), kind=kCustom, calls=%fused_computation.3 | custom fusion | bytes 65600 | tf_op jit(solution)/shard_map/jit(_take)/gather | solution.py:60
  50.1 0.7 broadcast_select_fusion
  50.8 3.9 %collective-permute-done.1 = bf16[1024,256]{0,1:T(8,128)(2,1)S(1)} collective-permute-done((bf16[1024,256]{0,1:T(8,128)(2,1)S(1)}, bf16[1024,256]{0,1:T(8,128)(2,1)S(1)}, u32[]{:S(2)}, u32[]{:S(2)}) %collective-permute-start.1) | collective-permute-done | bytes 524320 | tf_op jit(solution)/shard_map/ppermute | solution.py:20
  54.7 3.1 %multiply_reduce_fusion = f32[2048]{0:T(1024)S(1)} fusion(bf16[2048,1024]{1,0:T(8,128)(2,1)} %param.10), kind=kLoop, calls=%fused_computation.8 | loop fusion | flops 6289408 | bytes 4202496 | tf_op jit(solution)/shard_map/reduce_sum | solution.py:31
  57.8 0.7 gather_fusion.2
  58.5 6.3 %all_gather.13 = f32[10,1024]{1,0:T(8,128)S(1)} all-gather(f32[10,256]{1,0:T(8,128)S(1)} %copy-done.4), channel_id=1, replica_groups=mesh['centre'=8,'row'=4] {'row'}, dimensions={1}, use_global_device_ids=true | all-gather | bytes 51200 | tf_op jit(solution)/shard_map/all_gather | solution.py:57
  65.6 1.4 copy-done.1
  67.1 26.9 %multiply_multiply_fusion = f32[2048,1024]{0,1:T(8,128)} fusion(bf16[2048,1024]{1,0:T(8,128)(2,1)S(1)} %copy-done.1, f32[1024]{0:T(1024)S(1)} %add_sqrt_fusion.1, f32[2048]{0:T(1024)S(1)} %add_sqrt_fusion, bf16[1024,2048]{0,1:T(8,128)(2,1)S(1)} %constant_dynamic-update-slice_fusion, s32[]{:T(128)S(6)} %select_n.51), kind=kOutput, calls=%fused_computation.4 | convolution fusion | flops 4330618880 | bytes 14692356 | tf_op jit(solution)/shard_map/dot_general | solution.py:63
  93.9 9.3 %copy.14 = f32[2048,1024]{1,0:T(8,128)} copy(f32[2048,1024]{0,1:T(8,128)} %multiply_multiply_fusion) | data formatting | bytes 16777216 | tf_op jit(solution)/shard_map/mul | solution.py:40
  103.2 4.0 %gather_fusion.1 = f32[16,1024]{1,0:T(8,128)S(1)} fusion(f32[2048,1024]{1,0:T(8,128)} %copy.14, s32[1024]{0:T(1024)S(1)} %pad_clamp_fusion), kind=kCustom, calls=%fused_computation.1 | custom fusion | bytes 131136 | tf_op jit(solution)/shard_map/jit(_take)/gather | solution.py:66
  107.2 9.4 %convolution_bitcast_fusion = f32[10,1024]{1,0:T(8,128)S(1)} fusion(f32[2048,1024]{0,1:T(8,128)} %multiply_multiply_fusion, f32[10,2048]{1,0:T(8,128)S(1)} %copy-done), kind=kOutput, calls=%fused_computation.12 | convolution fusion | flops 251658240 | bytes 8511488 | tf_op jit(solution)/shard_map/dot_general | solution.py:65
  116.7 41.1 %psum.21 = f32[10,1024]{1,0:T(8,128)S(1)} all-reduce(f32[10,1024]{1,0:T(8,128)S(1)} %convolution_bitcast_fusion), channel_id=1, replica_groups=mesh['centre'=8,'row'=4] {'centre','row'}, use_global_device_ids=true, to_apply=%region_2.3 | all-reduce | flops 10240 | bytes 81920 | tf_op jit(solution)/shard_map/psum | solution.py:69
  158.2 39.4 %psum.22 = f32[10,128]{1,0:T(8,128)S(1)} all-reduce(f32[10,128]{1,0:T(8,128)S(1)} %fusion.35), channel_id=1, replica_groups=mesh['centre'=8,'row'=4] {'centre','row'}, use_global_device_ids=true, to_apply=%region_3.4 | all-reduce | flops 1280 | bytes 10240 | tf_op jit(solution)/shard_map/psum | solution.py:85
  197.8 31.3 %all_gather.14 = f32[10,512]{0,1:T(8,128)S(1)} all-gather(f32[10,16]{0,1:T(8,128)S(1)} %copy.15), channel_id=1, replica_groups=mesh['centre'=8,'row'=4] {'centre','row'}, dimensions={1}, use_global_device_ids=true | all-gather | bytes 21120 | tf_op jit(solution)/shard_map/all_gather | solution.py:81
  229.7 1.5 multiply_reduce_fusion.2
  231.2 1.6 fusion.3
  233.5 49.1 %psum.23 = f32[10,128]{1,0:T(8,128)S(1)} all-reduce(f32[10,128]{1,0:T(8,128)S(1)} %fusion.36), channel_id=1, replica_groups=mesh['centre'=8,'row'=4] {'centre','row'}, use_global_device_ids=true, to_apply=%region_5.6 | all-reduce | flops 1280 | bytes 10240 | tf_op jit(solution)/shard_map/psum | solution.py:85
  282.6 0.7 fusion.4
  (40 shorter events, 2.9 us)
Async XLA Ops:
  7.2 100.0 %copy-start = (f32[10,2048]{1,0:T(8,128)S(1)}, f32[10,2048]{1,0:T(8,128)}, u32[]{:S(2)}) copy-start(f32[10,2048]{1,0:T(8,128)} %param.11) | copy-start | bytes 245764
  7.2 222.5 %all-gather.2.cloned.1.call-start = ((), (), s32[]{:S(2)}) async-start(), calls=%async_computation | async-start | bytes 1081344 | tf_op jit(solution)/shard_map/all_gather | solution.py:73
  7.9 50.5 %copy-start.4 = (f32[10,256]{1,0:T(8,128)S(1)}, f32[10,256]{1,0:T(8,128)}, u32[]{:S(2)}) copy-start(f32[10,256]{1,0:T(8,128)} %param.9) | copy-start | bytes 30724
  37.5 8.6 %collective-permute-start = (bf16[1024,256]{0,1:T(8,128)(2,1)S(1)}, bf16[1024,256]{0,1:T(8,128)(2,1)S(1)}, u32[]{:S(2)}, u32[]{:S(2)}) collective-permute-start(bf16[1024,256]{0,1:T(8,128)(2,1)S(1)} %all_gather.12), channel_id=1, source_target_pairs={{0,1},{1,2},{2,3},{3,0},{4,5},{5,6},{6,7},{7,4},{8,9},{9,10},{10,1... | collective-permute-start | bytes 1572872 | tf_op jit(solution)/shard_map/ppermute | solution.py:20
  46.1 8.6 %collective-permute-start.1 = (bf16[1024,256]{0,1:T(8,128)(2,1)S(1)}, bf16[1024,256]{0,1:T(8,128)(2,1)S(1)}, u32[]{:S(2)}, u32[]{:S(2)}) collective-permute-start(bf16[1024,256]{0,1:T(8,128)(2,1)S(1)} %collective-permute-done), channel_id=1, source_target_pairs={{0,1},{1,2},{2,3},{3,0},{4,5},{5,6},{6,7},{7,4},{8,9},{9,10},{10,1... | collective-permute-start | bytes 1572872 | tf_op jit(solution)/shard_map/ppermute | solution.py:20
  54.7 10.1 %collective-permute-start.2 = (bf16[1024,256]{0,1:T(8,128)(2,1)S(1)}, bf16[1024,256]{0,1:T(8,128)(2,1)S(1)}, u32[]{:S(2)}, u32[]{:S(2)}) collective-permute-start(bf16[1024,256]{0,1:T(8,128)(2,1)S(1)} %collective-permute-done.1), channel_id=1, source_target_pairs={{0,1},{1,2},{2,3},{3,0},{4,5},{5,6},{6,7},{7,4},{8,9},{9,10},{10,1... | collective-permute-start | bytes 1572872 | tf_op jit(solution)/shard_map/ppermute | solution.py:20
  64.9 2.2 copy-start.1
  107.2 50.8 %copy-start.3 = (f32[16,128]{1,0:T(8,128)S(1)}, f32[16,128]{1,0:T(8,128)}, u32[]{:S(2)}) copy-start(f32[16,128]{1,0:T(8,128)} %param.13) | copy-start | bytes 24580
  107.2 124.0 %copy-start.2 = (bf16[16,1024]{1,0:T(8,128)(2,1)S(1)}, bf16[16,1024]{1,0:T(8,128)(2,1)}, u32[]{:S(2)}) copy-start(bf16[16,1024]{1,0:T(8,128)(2,1)} %broadcast_select_fusion) | copy-start | bytes 98308
Sparse Core Ops, SparseCore 0:
  50.9 53.4 all-gather.1
